TPU v7x, 256 devices: a whole 4x4x8 slice. The times are simulated.
256 devices in a mesh: dp: 16 (over y, x_lo, core), tensor: 16 (over x_hi, z).
Axes of the slice: x: 4 (x_hi: 2, x_lo: 2; x = x_hi * 2 + x_lo), y: 4, z: 8, core: 2. Of those that a mesh axis runs over, the one named last changes fastest.
Arguments:
- x_rows: bfloat16 [512, 8192], P('tensor', 'dp'), may hold values from -6 to 6
- grad_out: bfloat16 [512, 8192], P('tensor', 'dp'), may hold values from -6 to 6
- order: int32 [512], replicated, may hold values from 0 to 511, each once
- gate_t: bfloat16 [28672, 8192], P('tensor', 'dp'), may hold values from -0.0625 to 0.0625
- up_t: bfloat16 [28672, 8192], P('tensor', 'dp'), may hold values from -0.0625 to 0.0625
- down_w: bfloat16 [28672, 8192], P('tensor', 'dp'), may hold values from -0.0625 to 0.0625
Outputs:
- grad_x: bfloat16 [512, 8192], P('tensor', 'dp')
- grad_gate: bfloat16 [28672, 8192], P('tensor', 'dp')
- grad_up: bfloat16 [28672, 8192], P('tensor', 'dp')
- grad_down: bfloat16 [28672, 8192], P('tensor', 'dp')
Inputs may be any that keep to these rules, and one draw needn't show every extreme that they name: order is a permutation of 0 to 511.
All inputs are finite; a program needn't handle non-finite values.
Results may differ from a plain program's by a relative error of at most 0.0049.
Values may be sent and summed in bfloat16 or wider, within the bound.
A program may use at most 128 MiB of HBM per device.

v0:
```python
import jax
import jax.numpy as jnp
from jax import lax
from jax.sharding import PartitionSpec as P


def times_rows(left, weight):
    return lax.dot_general(
        left, weight, (((1,), (1,)), ((), ())), preferred_element_type=jnp.float32
    )


def per_device(x_rows, grad_out, order, gate_t, up_t, down_w):
    x_cols, dy_cols = (
        lax.all_gather(x_rows, "tensor", axis=0, tiled=True),
        lax.all_gather(grad_out, "tensor", axis=0, tiled=True),
    )
    xs = jnp.take(x_cols, order, axis=0)
    units = gate_t.shape[0]
    rows_x = xs
    rows_dy = dy_cols
    pre = lax.psum_scatter(
        jnp.concatenate(
            [times_rows(rows_x, gate_t), times_rows(rows_x, up_t), times_rows(rows_dy, down_w)],
            axis=1,
        ),
        "dp",
        scatter_dimension=0,
        tiled=True,
    )
    gate = pre[:, :units]
    up = pre[:, units : 2 * units]
    grad_hidden = pre[:, 2 * units :]
    sig = jax.nn.sigmoid(gate)
    act = gate * sig
    hidden = (act * up).astype(jnp.bfloat16)
    grad_pre_gate = (grad_hidden * up * sig * (1.0 + gate * (1.0 - sig))).astype(jnp.bfloat16)
    grad_pre_up = (grad_hidden * act).astype(jnp.bfloat16)
    hidden, grad_pre_gate, grad_pre_up = (hidden, grad_pre_gate, grad_pre_up)
    contribute_hidden = lax.all_gather(hidden, "dp", axis=0, tiled=True)
    contribute_grad_pre_gate = lax.all_gather(grad_pre_gate, "dp", axis=0, tiled=True)
    contribute_grad_pre_up = lax.all_gather(grad_pre_up, "dp", axis=0, tiled=True)
    rows_x = xs
    rows_dy = dy_cols
    acc_down = jnp.dot(contribute_hidden.T, rows_dy, preferred_element_type=jnp.float32)
    acc_gate = jnp.dot(contribute_grad_pre_gate.T, rows_x, preferred_element_type=jnp.float32)
    acc_up = jnp.dot(contribute_grad_pre_up.T, rows_x, preferred_element_type=jnp.float32)
    piece_cols = jnp.dot(contribute_grad_pre_gate, gate_t, preferred_element_type=jnp.float32)
    piece_cols = piece_cols + jnp.dot(
        contribute_grad_pre_up, up_t, preferred_element_type=jnp.float32
    )
    cols = piece_cols
    acc_down, acc_gate, acc_up, cols = (acc_down, acc_gate, acc_up, cols)
    stored = jnp.zeros_like(cols).at[order].set(cols)
    grad_x = lax.psum_scatter(stored, "tensor", scatter_dimension=0, tiled=True).astype(
        jnp.bfloat16
    )
    return (
        grad_x,
        acc_gate.astype(jnp.bfloat16),
        acc_up.astype(jnp.bfloat16),
        acc_down.astype(jnp.bfloat16),
    )


def solution(mesh):
    return jax.shard_map(
        per_device,
        mesh=mesh,
        in_specs=(
            P("tensor", "dp"),
            P("tensor", "dp"),
            P(),
            P("tensor", "dp"),
            P("tensor", "dp"),
            P("tensor", "dp"),
        ),
        out_specs=(P("tensor", "dp"), P("tensor", "dp"), P("tensor", "dp"), P("tensor", "dp")),
        check_vma=False,
    )
```

profile of v0, /device:TPU:1, one launch (start us, length us, event | category | flops | bytes accessed | tf_op | source)
XLA Modules:
  0.0 550.4 jit_solution(13249610129771851639)
XLA Ops:
  7.2 0.8 compare_and_fusion
  8.0 0.7 compare_select_fusion
  8.7 40.7 %all_gather.16 = bf16[512,512]{1,0:T(8,128)(2,1)S(1)} all-gather(bf16[32,512]{1,0:T(8,128)(2,1)} %param.7), channel_id=1, replica_groups=mesh['dp'=16,'tensor'=16] {'tensor'}, dimensions={0}, use_global_device_ids=true | all-gather | bytes 557056 | tf_op jit(solution)/shard_map/all_gather | solution.py:16
  49.4 31.8 %all_gather.15 = bf16[512,512]{1,0:T(8,128)(2,1)S(1)} all-gather(bf16[32,512]{1,0:T(8,128)(2,1)} %param.6), channel_id=1, replica_groups=mesh['dp'=16,'tensor'=16] {'tensor'}, dimensions={0}, use_global_device_ids=true | all-gather | bytes 557056 | tf_op jit(solution)/shard_map/all_gather | solution.py:15
  81.3 2.0 gather_fusion
  83.2 2.7 fusion.3
  85.9 1.2 fusion.4
  87.4 1.2 fusion.5
  88.6 4.5 pad_maximum_fusion
  93.2 135.4 %reduce-scatter.3.cloned.1.call-done = f32[32,5376]{1,0:T(8,128)} async-done(((f32[512,5376]{1,0:T(8,128)}), f32[32,5376]{1,0:T(8,128)}) %reduce-scatter.3.cloned.1.call-update) | async-done | bytes 688144 | tf_op jit(solution)/shard_map/reduce_scatter | solution.py:22
  228.6 2.0 multiply_convert_fusion
  230.6 0.7 all-gather.6.cloned.1.call-update
  231.4 0.5 all-gather.8.cloned.1.call-update
  231.9 36.1 %all-gather.4.cloned.1.call-done = bf16[512,1792]{1,0:T(8,128)(2,1)} async-done(((bf16[32,1792]{1,0:T(8,128)(2,1)}), bf16[512,1792]{1,0:T(8,128)(2,1)}) %all-gather.4.cloned.1.call-update) | async-done | bytes 1835024 | tf_op jit(solution)/shard_map/all_gather | solution.py:41
  268.1 3.6 fusion.6
  271.6 35.1 %all-gather.6.cloned.1.call-done = bf16[512,1792]{1,0:T(8,128)(2,1)} async-done(((bf16[32,1792]{1,0:T(8,128)(2,1)}), bf16[512,1792]{1,0:T(8,128)(2,1)}) %all-gather.6.cloned.1.call-update) | async-done | bytes 1835024 | tf_op jit(solution)/shard_map/all_gather | solution.py:42
  306.7 4.4 convolution_add_fusion
  311.1 3.9 scatter_custom_fusion
  315.1 30.2 %all-gather.8.cloned.1.call-done = bf16[512,1792]{1,0:T(8,128)(2,1)} async-done(((bf16[32,1792]{1,0:T(8,128)(2,1)}), bf16[512,1792]{1,0:T(8,128)(2,1)}) %all-gather.8.cloned.1.call-update) | async-done | bytes 1835024 | tf_op jit(solution)/shard_map/all_gather | solution.py:40
  345.3 4.0 convolution_convert_fusion
  349.3 2.4 convolution_convert_fusion.2
  351.7 2.4 convolution_convert_fusion.1
  354.1 188.3 %reduce-scatter.5.cloned.1.call-done = f32[32,512]{1,0:T(8,128)} async-done(((f32[512,512]{1,0:T(8,128)}), f32[32,512]{1,0:T(8,128)}) %reduce-scatter.5.cloned.1.call-update) | async-done | bytes 65552 | tf_op jit(solution)/shard_map/reduce_scatter | solution.py:55
  542.4 1.5 convert_element_type.23
  (17 shorter events, 0.6 us)
Async XLA Ops:
  7.2 78.7 %copy-start = (bf16[1792,512]{1,0:T(8,128)(2,1)S(1)}, bf16[1792,512]{1,0:T(8,128)(2,1)}, u32[]{:S(2)}) copy-start(bf16[1792,512]{1,0:T(8,128)(2,1)} %param.9) | copy-start | bytes 5505028
  7.2 221.4 %reduce-scatter.3.cloned.1.call-start = ((), (), s32[]{:S(2)}) async-start(), calls=%async_computation.2 | async-start | bytes 11698176 | tf_op jit(solution)/shard_map/reduce_scatter | solution.py:22
  85.9 1.5 copy-start.1
  93.1 174.9 %all-gather.4.cloned.1.call-start = ((), (), s32[]{:S(2)}) async-start(), calls=%async_computation.3 | async-start | bytes 1949696 | tf_op jit(solution)/shard_map/all_gather | solution.py:41
  230.6 76.2 %all-gather.6.cloned.1.call-start = ((), (), s32[]{:S(2)}) async-start(), calls=%async_computation.4 | async-start | bytes 1949696 | tf_op jit(solution)/shard_map/all_gather | solution.py:42
  231.3 113.9 %all-gather.8.cloned.1.call-start = ((), (), s32[]{:S(2)}) async-start(), calls=%async_computation.6 | async-start | bytes 1949696 | tf_op jit(solution)/shard_map/all_gather | solution.py:40
  231.9 310.5 %reduce-scatter.5.cloned.1.call-start = ((), (), s32[]{:S(2)}) async-start(), calls=%async_computation.5 | async-start | bytes 1114112 | tf_op jit(solution)/shard_map/reduce_scatter | solution.py:55
  345.3 4.0 copy-start.2
  349.3 2.4 copy-start.3
Sparse Core Ops, SparseCore 0:
  93.2 135.2 reduce-scatter.2
  231.0 37.0 all-gather.3
  270.5 36.1 all-gather.5
  309.0 36.1 all-gather.7
  348.9 193.4 reduce-scatter.4
where the time goes:
time: 555 us; the launch traced here: 550 us
  waiting for transfers between devices  426 us (77%)
  blocking collectives  72.5 us (13%)
  matrix products  21.9 us (4%)
  between operations  13.8 us (2%)
  other arithmetic  9.47 us (2%)
  local copies, waits for them, and re-layouts  6.2 us (1%)
    reduce_scatter x1, waiting for transfers between devices, per_device(): lax.psum_scatter(stored, 'tensor', scatter_dimension=0, tiled=True)  188 us
    reduce_scatter x1, waiting for transfers between devices, per_device(): lax.psum_scatter(jnp.concatenate([times_rows(rows_x, gate_t), times_rows(...  135 us
    all_gather x1, blocking collectives, per_device(): lax.all_gather(grad_out, 'tensor', axis=0, tiled=True)  40.7 us
    all_gather x1, waiting for transfers between devices, per_device(): lax.all_gather(grad_pre_gate, 'dp', axis=0, tiled=True)  36.1 us
    all_gather x1, waiting for transfers between devices, per_device(): lax.all_gather(grad_pre_up, 'dp', axis=0, tiled=True)  35.1 us
    all_gather x1, blocking collectives, per_device(): lax.all_gather(x_rows, 'tensor', axis=0, tiled=True)  31.8 us
    all_gather x1, waiting for transfers between devices, per_device(): contribute_hidden = lax.all_gather(hidden, 'dp', axis=0, tiled=True)  30.2 us
  transfers between devices with their start and end apart: 5, of which 5 were waited for; matrix products, arithmetic and copies ran while one was open for 4% of the time, Pallas kernels for 0%

commit v1 on v0

v1 whole, which is shorter than its diff:
```python
import functools

import jax
import jax.numpy as jnp
from jax import lax
from jax.experimental import pallas as pl
from jax.experimental.pallas import tpu as pltpu
from jax.sharding import PartitionSpec as P

MESH = pl.DeviceIdType.MESH
NY, NXL, NXH, NZ = 4, 2, 2, 8
CHUNKS = 7
ROWS = 128
SUB = 16
HALF_TOK = 256
TOK = 512
WIDE = 512
TB = 32
F32, BF16 = jnp.float32, jnp.bfloat16
Z_ORDER = (1, 7, 2, 6, 3, 5, 4)


def dot_nt(a, b):
    return lax.dot_general(a, b, (((1,), (1,)), ((), ())), preferred_element_type=F32)


def dot_nn(a, b):
    return lax.dot_general(a, b, (((1,), (0,)), ((), ())), preferred_element_type=F32)


def dot_tn(a, b):
    return lax.dot_general(a, b, (((0,), (0,)), ((), ())), preferred_element_type=F32)


def gated(pre):
    gate, up, grad_hidden = pre[0], pre[1], pre[2]
    sig = jax.nn.sigmoid(gate)
    act = gate * sig
    hidden = act * up
    grad_gate = grad_hidden * up * sig * (1.0 + gate * (1.0 - sig))
    grad_up = grad_hidden * act
    return jnp.stack([grad_gate, grad_up, hidden]).astype(BF16)


def kernel(
    x_hbm, dy_hbm, order_ref, wg, wu, wd,
    gx_out, gg_out, gu_out, gd_out,
    wall, wsib, xo, xs, dg, do, ds,
    pf_a, pf_b, pb_a, pb_b, rx_a, sb_a, ry_a, rb_b, s32_b, sb_b, rx_b,
    g_a, g_b, outs, gxa, gxb, gxr, gs32, gsb, gzr, gxf,
    c_send, c_recv, w_send, w_recv, l_sem, xz_send, xz_recv, xh_send, xh_recv,
    sib_send, sib_recv, o_sem, t_send, t_recv,
):
    dp = lax.axis_index("dp")
    tn = lax.axis_index("tensor")
    y, xl, k = dp // 4, (dp // 2) % 2, dp % 2
    xh, z = tn // 8, tn % 8

    def at(yy, xx, kk, hh, zz):
        return (yy * 4 + xx * 2 + kk, hh * 8 + zz)

    sibling = at(y, xl, 1 - k, xh, z)
    x_peer = at(y, 1 - xl, k, xh, z)
    h_peer = at(y, xl, k, 1 - xh, z)

    def y_peer(d):
        return at((y + d) % NY, xl, k, xh, z)

    def z_peer(d):
        return at(y, xl, k, xh, (z + d) % NZ)

    def rc(src, dst, send, recv, dev):
        return pltpu.make_async_remote_copy(
            src_ref=src, dst_ref=dst, send_sem=send, recv_sem=recv, device_id=dev, device_id_type=MESH
        )

    def load_w(j):
        src = (wg, wu, wd)[j]
        return pltpu.make_async_copy(src, wall.at[:, :, pl.ds(ROWS * j, ROWS)], l_sem.at[j])

    def send_w(j):
        src = (wg, wu, wd)[j]
        return rc(src.at[1 - k], wsib.at[:, pl.ds(ROWS * j, ROWS)], w_send.at[j], w_recv.at[j], sibling)

    def load_x():
        return pltpu.make_async_copy(x_hbm, xo.at[tn], l_sem.at[3])

    def load_dy():
        return pltpu.make_async_copy(dy_hbm, dg.at[tn], l_sem.at[4])

    def gather_z(j, d):
        src, dst = ((x_hbm, xo), (dy_hbm, dg))[j]
        return rc(src, dst.at[tn], xz_send.at[j, d], xz_recv.at[j, d], z_peer(d))

    def gather_h(j, d):
        dst = (xo, dg)[j]
        block = xh * NZ + (z + NZ - d) % NZ
        return rc(dst.at[block], dst.at[block], xh_send.at[j, d], xh_recv.at[j, d], h_peer)

    def swap_x():
        return rc(xo, xs, sib_send.at[0], sib_recv.at[0], sibling)

    def swap_dy():
        return rc(do, ds, sib_send.at[1], sib_recv.at[1], sibling)

    def cc(i, n, src, dst, dev):
        return rc(src, dst, c_send.at[i, n], c_recv.at[i, n], dev)

    def a1(i):
        return cc(i, 0, pb_a.at[i, :, 1 - xl], rx_a.at[i], x_peer)

    def a2(i, d):
        return cc(i, d, sb_a.at[i, :, (y + d) % NY], ry_a.at[i, d - 1], y_peer(d))

    def b1(i, d):
        return cc(i, 3 + d, pb_b.at[i, :, :, (y + d) % NY], rb_b.at[i, d - 1], y_peer(d))

    def b2(i):
        return cc(i, 7, sb_b.at[i], rx_b.at[i], x_peer)

    def ga1(i, d):
        ref = g_a.at[k, i, :, xl, y]
        return cc(i, 7 + d, ref, ref, y_peer(d))

    def ga2(i):
        ref = g_a.at[k, i, :, xl]
        return cc(i, 11, ref, ref, x_peer)

    def gb1(i):
        ref = g_b.at[k, i, :, xl, y]
        return cc(i, 12, ref, ref, x_peer)

    def gb2(i, d):
        ref = g_b.at[k, i, :, :, y]
        return cc(i, 12 + d, ref, ref, y_peer(d))

    def sw1(i):
        ref = g_a.at[k, i, :, xl]
        return cc(i, 16, ref, ref, sibling)

    def sw2(i):
        ref = g_a.at[k, i, :, 1 - xl]
        return cc(i, 17, ref, ref, sibling)

    def sw3(i):
        ref = g_b.at[k, i]
        return cc(i, 18, ref, ref, sibling)

    def write_out(i, h, j):
        dst = (gg_out, gu_out, gd_out)[j]
        return pltpu.make_async_copy(outs.at[h, i, pl.ds(ROWS * j, ROWS)], dst.at[h, i], o_sem.at[i, h, j])

    def tail_h():
        return rc(gxb.at[1 - xh], gxr, t_send.at[0], t_recv.at[0], h_peer)

    def tail_z(d):
        return rc(gsb.at[(z + d) % NZ], gzr.at[d - 1], t_send.at[d], t_recv.at[d], z_peer(d))

    load_x().start()
    load_dy().start()
    for j in range(3):
        load_w(j).start()
    barrier = pltpu.get_barrier_semaphore()
    partners = [sibling, x_peer, h_peer]
    partners += [y_peer(d) for d in range(1, NY)] + [z_peer(d) for d in range(1, NZ)]
    for dev in partners:
        pl.semaphore_signal(barrier, inc=1, device_id=dev, device_id_type=MESH)
    pl.semaphore_wait(barrier, len(partners))

    for j in range(2):
        for d in Z_ORDER:
            gather_z(j, d).start()
    for j in range(3):
        send_w(j).start()
    gxa[...] = jnp.zeros_like(gxa)

    for j in range(2):
        (load_x, load_dy)[j]().wait()
        gather_h(j, 0).start()
        for d in Z_ORDER:
            gather_z(j, d).wait_recv()
            gather_h(j, d).start()
        for d in range(NZ):
            gather_h(j, d).wait_recv()
        if j == 0:
            swap_x().start()
    rows = lax.broadcasted_iota(jnp.int32, (TOK, TOK), 0)
    place = jnp.where(rows == order_ref[...], 1.0, 0.0).astype(BF16)
    do[...] = dot_nn(place, dg[...].reshape(TOK, WIDE)).astype(BF16).reshape(NXH * NZ, TB, WIDE)
    swap_dy().start()
    for j in range(3):
        load_w(j).wait()
        send_w(j).wait_recv()
    swap_x().wait_recv()
    swap_dy().wait_recv()

    def flat(ref):
        return ref[...].reshape(TOK, WIDE)

    def forward(i):
        gu = dot_nt(wall[k, i, : 2 * ROWS], flat(xo)) + dot_nt(wsib[i, : 2 * ROWS], flat(xs))
        gh = dot_nt(wall[k, i, 2 * ROWS :], flat(do)) + dot_nt(wsib[i, 2 * ROWS :], flat(ds))
        for pf, pb, lo in ((pf_a, pb_a, 0), (pf_b, pb_b, HALF_TOK)):
            part_gu = gu[:, lo : lo + HALF_TOK].reshape(2, NXL, NY, SUB, HALF_TOK)
            part_gh = gh[:, lo : lo + HALF_TOK].reshape(NXL, NY, SUB, HALF_TOK)
            pf[i, 0:2] = part_gu
            pf[i, 2] = part_gh
            pb[i, 0:2] = part_gu.astype(BF16)
            pb[i, 2] = part_gh.astype(BF16)
        a1(i).start()
        for d in range(1, NY):
            b1(i, d).start()

    def reduce_one(i):
        a1(i).wait_recv()
        sb_a[i] = (pf_a[i, :, xl] + rx_a[i].astype(F32)).astype(BF16)
        for d in range(1, NY):
            a2(i, d).start()
        total = pf_b[i, :, :, y]
        for d in range(1, NY):
            b1(i, d).wait_recv()
            total = total + rb_b[i, d - 1].astype(F32)
        s32_b[i] = total
        sb_b[i] = s32_b[i, :, 1 - xl].astype(BF16)
        b2(i).start()

    def reduce_two(i):
        total = pf_a[i, :, xl, y] + rx_a[i, :, y].astype(F32)
        for d in range(1, NY):
            a2(i, d).wait_recv()
            total = total + ry_a[i, d - 1].astype(F32)
        g_a[k, i, :, xl, y] = gated(total)
        for d in range(1, NY):
            ga1(i, d).start()
        b2(i).wait_recv()
        g_b[k, i, :, xl, y] = gated(s32_b[i, :, xl] + rx_b[i].astype(F32))
        gb1(i).start()

    def gather_one(i):
        gb1(i).wait_recv()
        for d in range(1, NY):
            gb2(i, d).start()
        for d in range(1, NY):
            ga1(i, d).wait_recv()
        ga2(i).start()
        sw1(i).start()

    def gather_two(i):
        ga2(i).wait_recv()
        sw2(i).start()
        for d in range(1, NY):
            gb2(i, d).wait_recv()
        sw3(i).start()

    def backward(i):
        for sw in (sw1, sw2, sw3):
            sw(i).wait_recv()
        for h in range(2):
            for n, g in ((0, g_a), (1, g_b)):
                gxa[n] += dot_tn(
                    g[h, i, 0:2].reshape(2 * ROWS, HALF_TOK), wall[h, i, : 2 * ROWS]
                ).reshape(NZ, TB, WIDE)

    def backward_w(i):
        half = (NZ * TB, WIDE)
        for h in range(2):
            gu = dot_nn(g_a[h, i, 0:2].reshape(2 * ROWS, HALF_TOK), xo[:NZ].reshape(half))
            gu = gu + dot_nn(g_b[h, i, 0:2].reshape(2 * ROWS, HALF_TOK), xo[NZ:].reshape(half))
            gd = dot_nn(g_a[h, i, 2].reshape(ROWS, HALF_TOK), do[:NZ].reshape(half))
            gd = gd + dot_nn(g_b[h, i, 2].reshape(ROWS, HALF_TOK), do[NZ:].reshape(half))
            outs[h, i, : 2 * ROWS] = gu.astype(BF16)
            outs[h, i, 2 * ROWS :] = gd.astype(BF16)
            for j in range(3):
                write_out(i, h, j).start()

    steps = (forward, reduce_one, reduce_two, gather_one, gather_two, backward)
    after = (0, 1, 2, 3, 4, 5)

    def turn(it, _):
        for step, lag in zip(steps, after):
            i = it - lag

            @pl.when((i >= 0) & (i < CHUNKS))
            def _():
                step(i)

        i = it - after[-1]

        @pl.when((i >= 0) & (i < CHUNKS - 1))
        def _():
            backward_w(i)

        return 0

    lax.fori_loop(0, CHUNKS + after[-1], turn, 0)

    gxb[...] = gxa[...].astype(BF16)
    tail_h().start()
    backward_w(CHUNKS - 1)
    tail_h().wait_recv()
    gs32[...] = gxa[xh] + gxr[...].astype(F32)
    gsb[...] = gs32[...].astype(BF16)
    for d in Z_ORDER:
        tail_z(d).start()
    total = gs32[z]
    for d in Z_ORDER:
        tail_z(d).wait_recv()
        total = total + gzr[d - 1].astype(F32)
    gxf[...] = total.astype(BF16)
    done = pltpu.make_async_copy(gxf, gx_out, l_sem.at[5])
    done.start()

    for j in range(3):
        send_w(j).wait_send()
    for j in range(2):
        for d in range(1, NZ):
            gather_z(j, d).wait_send()
        for d in range(NZ):
            gather_h(j, d).wait_send()
    swap_x().wait_send()
    swap_dy().wait_send()

    def drain(i, _):
        for c in (a1(i), b2(i), ga2(i), gb1(i), sw1(i), sw2(i), sw3(i)):
            c.wait_send()
        for d in range(1, NY):
            for c in (a2(i, d), b1(i, d), ga1(i, d), gb2(i, d)):
                c.wait_send()
        for h in range(2):
            for j in range(3):
                write_out(i, h, j).wait()
        return 0

    lax.fori_loop(0, CHUNKS, drain, 0)
    tail_h().wait_send()
    for d in range(1, NZ):
        tail_z(d).wait_send()
    done.wait()


def per_device(x_rows, grad_out, order, gate_t, up_t, down_w):
    weight = (2, CHUNKS, ROWS, WIDE)
    any_spec = pl.BlockSpec(memory_space=pl.ANY)
    dma = pltpu.SemaphoreType.DMA
    n = CHUNKS
    vm = pltpu.VMEM
    scratch = [
        vm((2, n, 3 * ROWS, WIDE), BF16),
        vm((n, 3 * ROWS, WIDE), BF16),
        vm((16, TB, WIDE), BF16),
        vm((16, TB, WIDE), BF16),
        vm((16, TB, WIDE), BF16),
        vm((16, TB, WIDE), BF16),
        vm((16, TB, WIDE), BF16),
        vm((n, 3, NXL, NY, SUB, HALF_TOK), F32),
        vm((n, 3, NXL, NY, SUB, HALF_TOK), F32),
        vm((n, 3, NXL, NY, SUB, HALF_TOK), BF16),
        vm((n, 3, NXL, NY, SUB, HALF_TOK), BF16),
        vm((n, 3, NY, SUB, HALF_TOK), BF16),
        vm((n, 3, NY, SUB, HALF_TOK), BF16),
        vm((n, 3, 3, SUB, HALF_TOK), BF16),
        vm((n, 3, 3, NXL, SUB, HALF_TOK), BF16),
        vm((n, 3, NXL, SUB, HALF_TOK), F32),
        vm((n, 3, SUB, HALF_TOK), BF16),
        vm((n, 3, SUB, HALF_TOK), BF16),
        vm((2, n, 3, NXL, NY, SUB, HALF_TOK), BF16),
        vm((2, n, 3, NXL, NY, SUB, HALF_TOK), BF16),
        vm((2, n, 3 * ROWS, WIDE), BF16),
        vm((NXH, NZ, TB, WIDE), F32),
        vm((NXH, NZ, TB, WIDE), BF16),
        vm((NZ, TB, WIDE), BF16),
        vm((NZ, TB, WIDE), F32),
        vm((NZ, TB, WIDE), BF16),
        vm((NZ - 1, TB, WIDE), BF16),
        vm((TB, WIDE), BF16),
        dma((n, 19)), dma((n, 19)),
        dma((3,)), dma((3,)),
        dma((6,)),
        dma((2, NZ)), dma((2, NZ)),
        dma((2, NZ)), dma((2, NZ)),
        dma((2,)), dma((2,)),
        dma((n, 2, 3)),
        dma((NZ,)), dma((NZ,)),
    ]
    out = pl.pallas_call(
        kernel,
        out_shape=[jax.ShapeDtypeStruct((TB, WIDE), BF16)]
        + [jax.ShapeDtypeStruct(weight, BF16)] * 3,
        in_specs=[any_spec, any_spec, pl.BlockSpec(memory_space=pltpu.VMEM)] + [any_spec] * 3,
        out_specs=[any_spec] * 4,
        scratch_shapes=scratch,
        compiler_params=pltpu.CompilerParams(
            collective_id=0, has_side_effects=True, vmem_limit_bytes=56 * 2**20
        ),
        name="ffn_backward",
    )(
        x_rows, grad_out, order.reshape(1, TOK),
        gate_t.reshape(weight), up_t.reshape(weight), down_w.reshape(weight),
    )
    full = gate_t.shape
    return out[0], out[1].reshape(full), out[2].reshape(full), out[3].reshape(full)


def solution(mesh):
    return jax.shard_map(
        per_device,
        mesh=mesh,
        in_specs=(
            P("tensor", "dp"),
            P("tensor", "dp"),
            P(),
            P("tensor", "dp"),
            P("tensor", "dp"),
            P("tensor", "dp"),
        ),
        out_specs=(P("tensor", "dp"), P("tensor", "dp"), P("tensor", "dp"), P("tensor", "dp")),
        check_vma=False,
    )
```

time: 555 us -> 114 us (0.21)
  waiting for transfers between devices: 426 us -> 0 us
  Pallas kernels: 0 us -> 105 us
  blocking collectives: 72.5 us -> 0 us
  matrix products: 21.9 us -> 0 us
  between operations: 13.8 us -> 0.64 us
  other arithmetic: 9.47 us -> 0 us
    reduce_scatter x2 -> x0, waiting for transfers between devices: 324 us -> none  [the longest x1 188 us: per_device(): lax.psum_scatter(stored, 'tensor', scatter_dimension=0, tiled=True)]
    pallas_call x0 -> x1, Pallas kernels: none -> 105 us  [per_device(): pl.pallas_call(kernel, out_shape=[jax.ShapeDtypeStruct((TB, WIDE), BF16)]...]
    all_gather x3 -> x0, waiting for transfers between devices: 101 us -> none  [the longest x1 36.1 us: per_device(): lax.all_gather(grad_pre_gate, 'dp', axis=0, tiled=True)]
    all_gather x2 -> x0, blocking collectives: 72.5 us -> none  [the longest x1 40.7 us: per_device(): lax.all_gather(grad_out, 'tensor', axis=0, tiled=True)]
    dot_general x8 -> x0, matrix products: 21.9 us -> none  [the longest x3 5.02 us: times_rows(): lax.dot_general(left, weight, (((1,), (1,)), ((), ())), preferred_element...]
    unnamed x8, local copies, waits for them, and re-layouts: 0.33 us -> 7.75 us
  transfers between devices with their start and end apart: 5 -> 0, of which waited for: 5 -> 0; matrix products, arithmetic and copies ran while one was open for 4% -> 0% of each run, Pallas kernels for 0% -> 0%
where the time goes in v1:
time: 114 us
  Pallas kernels  105 us (92%)
  local copies, waits for them, and re-layouts  7.75 us (7%)
    pallas_call x1, Pallas kernels, per_device(): pl.pallas_call(kernel, out_shape=[jax.ShapeDtypeStruct((TB, WIDE), BF16)]...  105 us
    unnamed x8, local copies, waits for them, and re-layouts  7.75 us

profile of v1, /device:TPU:1, one launch (start us, length us, event | category | flops | bytes accessed | tf_op | source)
XLA Modules:
  0.0 113.9 jit_solution(107639387697363776)
XLA Ops:
  0.6 105.5 %ffn_backward.1 = (bf16[32,512]{1,0:T(8,128)(2,1)}, bf16[2,7,128,512]{3,2,1,0:T(8,128)(2,1)}, bf16[2,7,128,512]{3,2,1,0:T(8,128)(2,1)}, bf16[2,7,128,512]{3,2,1,0:T(8,128)(2,1)}) custom-call(bf16[32,512]{1,0:T(8,128)(2,1)} %x_hbm.1, bf16[32,512]{1,0:T(8,128)(2,1)} %dy_hbm.1, s32[1,512]{1,0:T(1,128)} %bitcast.13, bf16[2,7,128,512]{3,2,1,0:T(8,128)(2,1)} %bitcast.10, ...), custom_call_target="tpu_custom_call" | custom-call | tf_op jit(solution)/shard_map/ffn_backward/pallas_call | solution.py:385
  106.1 1.4 %copy.14 = bf16[32,512]{1,0:T(8,128)(2,1)} copy(bf16[32,512]{1,0:T(8,128)(2,1)} %get-tuple-element.16) | data formatting | bytes 65536
  107.5 0.0 copy-start.1
  107.5 3.0 %copy.15 = bf16[1792,512]{1,0:T(8,128)(2,1)} copy(bf16[1792,512]{1,0:T(8,128)(2,1)} %bitcast.9) | data formatting | bytes 3670016
  110.5 0.0 copy-done.1
  110.5 0.0 copy-start
  110.5 1.2 %copy.16 = bf16[1792,512]{1,0:T(8,128)(2,1)} copy(bf16[1792,512]{1,0:T(8,128)(2,1)S(1)} %bitcast.8) | data formatting | bytes 3670016
  111.7 0.9 copy-done
  112.6 1.2 %copy.17 = bf16[1792,512]{1,0:T(8,128)(2,1)} copy(bf16[1792,512]{1,0:T(8,128)(2,1)S(1)} %bitcast.7) | data formatting | bytes 3670016
Async XLA Ops:
  107.5 3.0 %copy-start.1 = (bf16[2,7,128,512]{3,2,1,0:T(8,128)(2,1)S(1)}, bf16[2,7,128,512]{3,2,1,0:T(8,128)(2,1)}, u32[]{:S(2)}) copy-start(bf16[2,7,128,512]{3,2,1,0:T(8,128)(2,1)} %get-tuple-element.10) | copy-start | bytes 5505028
  110.5 2.2 %copy-start = (bf16[2,7,128,512]{3,2,1,0:T(8,128)(2,1)S(1)}, bf16[2,7,128,512]{3,2,1,0:T(8,128)(2,1)}, u32[]{:S(2)}) copy-start(bf16[2,7,128,512]{3,2,1,0:T(8,128)(2,1)} %get-tuple-element.11) | copy-start | bytes 5505028

commit v2 on v0

v2 whole, which is shorter than its diff:
```python
from types import SimpleNamespace

import jax
import jax.numpy as jnp
from jax import lax
from jax.experimental import pallas as pl
from jax.experimental.pallas import tpu as pltpu
from jax.sharding import PartitionSpec as P

MESH = pl.DeviceIdType.MESH
NY, NXL, NXH, NZ = 4, 2, 2, 8
CHUNKS = 7
ROWS = 128
SUB = 16
HALF = 256
TOK = 512
WIDE = 512
TB = 32
F32, BF16 = jnp.float32, jnp.bfloat16
Z_ORDER = (1, 7, 2, 6, 3, 5, 4)
Y_ALL = (1, 3, 2)
WEIGHT = (2, CHUNKS, ROWS, WIDE)


def dot_nt(a, b):
    return lax.dot_general(a, b, (((1,), (1,)), ((), ())), preferred_element_type=F32)


def dot_nn(a, b):
    return lax.dot_general(a, b, (((1,), (0,)), ((), ())), preferred_element_type=F32)


def dot_tn(a, b):
    return lax.dot_general(a, b, (((0,), (0,)), ((), ())), preferred_element_type=F32)


def scratch_plan():
    n = CHUNKS
    cell = (SUB, HALF)
    plan = [
        ("wall", (2, n, 3 * ROWS, WIDE), BF16),
        ("wsib", (n, 3 * ROWS, WIDE), BF16),
        ("xo", (NXH, NZ, TB, WIDE), BF16),
        ("xs", (NXH, NZ, TB, WIDE), BF16),
        ("dg", (NXH, NZ, TB, WIDE), BF16),
        ("do", (NXH, NZ, TB, WIDE), BF16),
        ("ds", (NXH, NZ, TB, WIDE), BF16),
        ("place", (TOK, TOK), BF16),
    ]
    for s, nf in (("u", 2), ("d", 1)):
        grid = (n, nf, NXL, NY) + cell
        plan += [
            (s + "_pf_a", grid, F32),
            (s + "_pf_b", grid, F32),
            (s + "_pb_a", grid, BF16),
            (s + "_pb_b", grid, BF16),
            (s + "_rx_a", (n, nf, NY) + cell, BF16),
            (s + "_sb_a", (n, nf, NY) + cell, BF16),
            (s + "_ry_a", (n, 3, nf) + cell, BF16),
            (s + "_r0_b", (n, 2, nf) + cell, BF16),
            (s + "_f_b", (n, 2, nf, NXL) + cell, BF16),
            (s + "_r1_b", (n, 2, nf, NXL) + cell, BF16),
            (s + "_s_b", (n, nf, NXL) + cell, F32),
            (s + "_sb_b", (n, nf) + cell, BF16),
            (s + "_rx_b", (n, nf) + cell, BF16),
            (s + "_send", (n, 9), None),
            (s + "_recv", (n, 9), None),
        ]
    plan += [
        ("t_a", (n, 2) + cell, F32),
        ("t_b", (n, 2) + cell, F32),
        ("g_a", (2, n, 2, NXL, NY) + cell, BF16),
        ("g_b", (2, n, 2, NXL, NY) + cell, BF16),
        ("h_a", (2, n, NXL, NY) + cell, BF16),
        ("h_b", (2, n, NXL, NY) + cell, BF16),
        ("gxa", (NXH, NZ, TB, WIDE), F32),
        ("es", (NXH, TB, HALF), F32),
        ("esr", (TB, HALF), F32),
        ("gxb", (2, NXH, NZ, TB, HALF), BF16),
        ("gxr", (NZ, TB, HALF), BF16),
        ("gs", (NZ, TB, HALF), F32),
        ("gsb", (NZ, TB, HALF), BF16),
        ("gz1", (NZ - 1, TB, HALF), BF16),
        ("gz2", (NZ - 1, NXH, TB, HALF), BF16),
        ("g_send", (n, 12), None),
        ("g_recv", (n, 12), None),
        ("h_send", (11,), None),
        ("h_recv", (11,), None),
        ("w_send", (3,), None),
        ("w_recv", (3,), None),
        ("l_sem", (5,), None),
        ("xz_send", (2, NZ), None),
        ("xz_recv", (2, NZ), None),
        ("xh_send", (NZ + 1,), None),
        ("xh_recv", (NZ + 1,), None),
        ("sib_send", (3,), None),
        ("sib_recv", (3,), None),
        ("t_send", (2 * NZ,), None),
        ("t_recv", (2 * NZ,), None),
    ]
    return plan


def kernel(x_hbm, dy_hbm, order_ref, wg, wu, wd, gx_ref, outs, *scratch):
    m = SimpleNamespace(**{p[0]: ref for p, ref in zip(scratch_plan(), scratch)})
    dp = lax.axis_index("dp")
    tn = lax.axis_index("tensor")
    y, xl, k = dp // 4, (dp // 2) % 2, dp % 2
    xh, z = tn // NZ, tn % NZ

    def at(yy, xx, kk, hh, zz):
        return (yy * 4 + xx * 2 + kk, hh * NZ + zz)

    sibling = at(y, xl, 1 - k, xh, z)
    x_peer = at(y, 1 - xl, k, xh, z)
    h_peer = at(y, xl, k, 1 - xh, z)

    def y_at(d):
        return (y + d) % NY

    def y_peer(d):
        return at(y_at(d), xl, k, xh, z)

    def z_peer(d):
        return at(y, xl, k, xh, (z + d) % NZ)

    def rc(src, dst, send, recv, dev):
        return pltpu.make_async_remote_copy(
            src_ref=src, dst_ref=dst, send_sem=send, recv_sem=recv, device_id=dev, device_id_type=MESH
        )

    def load_w(j):
        return pltpu.make_async_copy(
            (wg, wu, wd)[j], m.wall.at[:, :, pl.ds(ROWS * j, ROWS)], m.l_sem.at[j]
        )

    def send_w(j):
        dst = m.wsib.at[:, pl.ds(ROWS * j, ROWS)]
        return rc((wg, wu, wd)[j].at[1 - k], dst, m.w_send.at[j], m.w_recv.at[j], sibling)

    def load_x():
        return pltpu.make_async_copy(x_hbm, m.xo.at[xh, z], m.l_sem.at[3])

    def load_dy():
        return pltpu.make_async_copy(dy_hbm, m.dg.at[xh, z], m.l_sem.at[4])

    def x_z(d):
        return rc(x_hbm, m.xo.at[xh, z], m.xz_send.at[0, d], m.xz_recv.at[0, d], z_peer(d))

    def x_h(d):
        block = m.xo.at[xh, (z + NZ - d) % NZ]
        return rc(block, block, m.xh_send.at[d], m.xh_recv.at[d], h_peer)

    def dy_h():
        return rc(dy_hbm, m.dg.at[xh, z], m.xh_send.at[NZ], m.xh_recv.at[NZ], h_peer)

    def dy_z(d):
        pair = m.dg.at[:, z]
        return rc(pair, pair, m.xz_send.at[1, d], m.xz_recv.at[1, d], z_peer(d))

    def swap_x(part):
        half = (xh, 1 - xh)[part]
        return rc(m.xo.at[half], m.xs.at[half], m.sib_send.at[part], m.sib_recv.at[part], sibling)

    def swap_dy():
        return rc(m.do, m.ds, m.sib_send.at[2], m.sib_recv.at[2], sibling)

    def stream(s, nf):
        pre = s + "_"
        q = SimpleNamespace(
            **{key[len(pre) :]: ref for key, ref in vars(m).items() if key.startswith(pre)}
        )

        def cc(i, c, src, dst, dev):
            return rc(src, dst, q.send.at[i, c], q.recv.at[i, c], dev)

        def a1(i):
            return cc(i, 0, q.pb_a.at[i, :, 1 - xl], q.rx_a.at[i], x_peer)

        def a2(i, d):
            return cc(i, d, q.sb_a.at[i, :, y_at(d)], q.ry_a.at[i, d - 1], y_peer(d))

        def b0(i, w):
            return cc(i, 4 + w, q.pb_b.at[i, :, w, y_at(2)], q.r0_b.at[i, w], y_peer((1, 3)[w]))

        def b1(i, w):
            return cc(i, 6 + w, q.f_b.at[i, w], q.r1_b.at[i, w], y_peer((1, 3)[w]))

        def b2(i):
            return cc(i, 8, q.sb_b.at[i], q.rx_b.at[i], x_peer)

        def begin(i, parts):
            for pf, pb, lo in ((q.pf_a, q.pb_a, 0), (q.pf_b, q.pb_b, HALF)):
                part = parts[:, lo : lo + HALF].reshape(nf, NXL, NY, SUB, HALF)
                pf[i] = part
                pb[i] = part.astype(BF16)
            a1(i).start()
            for w in range(2):
                b0(i, w).start()

        def first(i):
            for w in range(2):
                b0(i, w).wait_recv()
                to = y_at((1, 3)[w])
                q.f_b[i, w, :, w] = (q.pf_b[i, :, w, to] + q.r0_b[i, w].astype(F32)).astype(BF16)
                q.f_b[i, w, :, 1 - w] = q.pb_b[i, :, 1 - w, to]
                b1(i, w).start()
            a1(i).wait_recv()
            q.sb_a[i] = (q.pf_a[i, :, xl] + q.rx_a[i].astype(F32)).astype(BF16)
            for d in Y_ALL:
                a2(i, d).start()

        def sum_a(i):
            total = q.pf_a[i, :, xl, y] + q.rx_a[i, :, y].astype(F32)
            for d in Y_ALL:
                a2(i, d).wait_recv()
                total = total + q.ry_a[i, d - 1].astype(F32)
            return total

        def second_b(i):
            total = q.pf_b[i, :, :, y]
            for w in range(2):
                b1(i, w).wait_recv()
                total = total + q.r1_b[i, w].astype(F32)
            q.s_b[i] = total
            q.sb_b[i] = q.s_b[i, :, 1 - xl].astype(BF16)
            b2(i).start()

        def sum_b(i):
            b2(i).wait_recv()
            return q.s_b[i, :, xl] + q.rx_b[i].astype(F32)

        def sent(i):
            cs = [a1(i), b2(i)] + [a2(i, d) for d in Y_ALL]
            return cs + [b(i, w) for b in (b0, b1) for w in range(2)]

        return SimpleNamespace(
            begin=begin, first=first, sum_a=sum_a, second_b=second_b, sum_b=sum_b, sent=sent
        )

    up_stream, dy_stream = stream("u", 2), stream("d", 1)

    def cg(i, c, src, dev):
        return rc(src, src, m.g_send.at[i, c], m.g_recv.at[i, c], dev)

    def ga1(i, d):
        return cg(i, d - 1, m.g_a.at[k, i, :, xl, y], y_peer(d))

    def ga2(i):
        return cg(i, 3, m.g_a.at[k, i, :, xl], x_peer)

    def gb1(i):
        return cg(i, 4, m.g_b.at[k, i, :, xl, y], x_peer)

    def gb2(i, w):
        return cg(i, 5 + w, m.g_b.at[k, i, :, :, y], y_peer((1, 3)[w]))

    def gb3(i, w):
        return cg(i, 7 + w, m.g_b.at[k, i, :, w, y_at((3, 1)[w])], y_peer((1, 3)[w]))

    def sw(i, part):
        src = (m.g_a.at[k, i, :, xl], m.g_a.at[k, i, :, 1 - xl], m.g_b.at[k, i])[part]
        return cg(i, 9 + part, src, sibling)

    def ch(c, src, dev):
        return rc(src, src, m.h_send.at[c], m.h_recv.at[c], dev)

    def ha1(d):
        return ch(d - 1, m.h_a.at[k, :, xl, y], y_peer(d))

    def ha2():
        return ch(3, m.h_a.at[k, :, xl], x_peer)

    def hb1():
        return ch(4, m.h_b.at[k, :, xl, y], x_peer)

    def hb2(d):
        return ch(4 + d, m.h_b.at[k, :, :, y], y_peer(d))

    def hsw(part):
        src = (m.h_a.at[k, :, xl], m.h_a.at[k, :, 1 - xl], m.h_b.at[k])[part]
        return ch(8 + part, src, sibling)

    def ct(c, src, dst, dev):
        return rc(src, dst, m.t_send.at[c], m.t_recv.at[c], dev)

    def tail_h():
        return ct(0, m.gxb.at[0, 1 - xh], m.gxr, h_peer)

    def tail_z1(d):
        return ct(d, m.gsb.at[(z + d) % NZ], m.gz1.at[d - 1], z_peer(d))

    def tail_z2(d):
        return ct(NZ + d, m.gxb.at[1, :, (z + d) % NZ], m.gz2.at[d - 1], z_peer(d))

    def tail_h2():
        return ct(NZ, m.es.at[1 - xh], m.esr, h_peer)

    load_x().start()
    load_dy().start()
    for j in range(3):
        load_w(j).start()
    barrier = pltpu.get_barrier_semaphore()
    partners = [z_peer(d) for d in range(1, NZ)] + [y_peer(d) for d in range(1, NY)]
    partners += [h_peer, x_peer, sibling]
    for dev in partners:
        pl.semaphore_signal(barrier, inc=1, device_id=dev, device_id_type=MESH)
    pl.semaphore_wait(barrier, len(partners))

    for d in Z_ORDER:
        x_z(d).start()
    load_x().wait()
    x_h(0).start()
    dy_h().start()
    for j in range(3):
        send_w(j).start()
    m.gxa[...] = jnp.zeros_like(m.gxa)
    rows = lax.broadcasted_iota(jnp.int32, (TOK, TOK), 0)
    m.place[...] = jnp.where(rows == order_ref[...], 1.0, 0.0).astype(BF16)
    for d in Z_ORDER:
        x_z(d).wait_recv()
        x_h(d).start()
    swap_x(0).start()
    load_dy().wait()
    dy_h().wait_recv()
    for d in Z_ORDER:
        dy_z(d).start()
    for d in range(NZ):
        x_h(d).wait_recv()
    swap_x(1).start()
    for j in range(2):
        load_w(j).wait()
        send_w(j).wait_recv()
    for part in range(2):
        swap_x(part).wait_recv()

    def flat(ref):
        return ref[...].reshape(TOK, WIDE)

    def prepare_dy():
        for d in Z_ORDER:
            dy_z(d).wait_recv()
        m.do[...] = dot_nn(m.place[...], flat(m.dg)).astype(BF16).reshape(NXH, NZ, TB, WIDE)
        swap_dy().start()

    def forward_u(i):
        up_stream.begin(
            i,
            dot_nt(m.wall[k, i, : 2 * ROWS], flat(m.xo)) + dot_nt(m.wsib[i, : 2 * ROWS], flat(m.xs)),
        )

    def forward_d(i):
        dy_stream.begin(
            i,
            dot_nt(m.wall[k, i, 2 * ROWS :], flat(m.do)) + dot_nt(m.wsib[i, 2 * ROWS :], flat(m.ds)),
        )

    def hidden_of(i, total, t, h):
        t[i] = total
        gate, up = total[0], total[1]
        h[k, i, xl, y] = (gate * jax.nn.sigmoid(gate) * up).astype(BF16)

    def second_u(i):
        hidden_of(i, up_stream.sum_a(i), m.t_a, m.h_a)
        up_stream.second_b(i)

    def third_u(i):
        hidden_of(i, up_stream.sum_b(i), m.t_b, m.h_b)

    def gated(i, grad_hidden, t, g):
        gate, up = t[i, 0], t[i, 1]
        sig = jax.nn.sigmoid(gate)
        grad_gate = grad_hidden * up * sig * (1.0 + gate * (1.0 - sig))
        grad_up = grad_hidden * (gate * sig)
        g[k, i, 0, xl, y] = grad_gate.astype(BF16)
        g[k, i, 1, xl, y] = grad_up.astype(BF16)

    def second_d(i):
        gated(i, dy_stream.sum_a(i)[0], m.t_a, m.g_a)
        for d in Y_ALL:
            ga1(i, d).start()
        dy_stream.second_b(i)

    def third_d(i):
        gated(i, dy_stream.sum_b(i)[0], m.t_b, m.g_b)
        gb1(i).start()

    def gather_a1(i):
        for d in Y_ALL:
            ga1(i, d).wait_recv()
        ga2(i).start()
        sw(i, 0).start()

    def gather_b1(i):
        gb1(i).wait_recv()
        for w in range(2):
            gb2(i, w).start()

    def gather_a2(i):
        ga2(i).wait_recv()
        sw(i, 1).start()

    def gather_b2(i):
        for w in range(2):
            gb2(i, w).wait_recv()
            gb3(i, w).start()

    def gather_b3(i):
        for w in range(2):
            gb3(i, w).wait_recv()
        sw(i, 2).start()

    def backward(i, p, g):
        for h in range(2):
            m.gxa[p] += dot_tn(
                g[h, i].reshape(2 * ROWS, HALF), m.wall[h, i, : 2 * ROWS]
            ).reshape(NZ, TB, WIDE)

    def backward_a(i):
        for part in range(2):
            sw(i, part).wait_recv()
        backward(i, 0, m.g_a)

    def backward_b(i):
        sw(i, 2).wait_recv()
        backward(i, 1, m.g_b)

    def backward_w(i):
        for h in range(2):
            gu = dot_nn(m.g_a[h, i].reshape(2 * ROWS, HALF), m.xo[0].reshape(HALF, WIDE))
            gu = gu + dot_nn(m.g_b[h, i].reshape(2 * ROWS, HALF), m.xo[1].reshape(HALF, WIDE))
            outs[h, i, : 2 * ROWS] = gu.astype(BF16)

    def backward_d(i):
        for h in range(2):
            gd = dot_nn(m.h_a[h, i].reshape(ROWS, HALF), m.do[0].reshape(HALF, WIDE))
            gd = gd + dot_nn(m.h_b[h, i].reshape(ROWS, HALF), m.do[1].reshape(HALF, WIDE))
            outs[h, i, 2 * ROWS :] = gd.astype(BF16)

    end = CHUNKS - 1

    def each(*steps, lo=0, hi=CHUNKS):
        most = max(lag for _, lag in steps)

        def turn(it, _):
            for step, lag in steps:
                i = it - lag
                if most == 0:
                    step(i)
                    continue

                @pl.when((i >= lo) & (i < hi))
                def _():
                    step(i)

            return 0

        lax.fori_loop(lo, hi + most, turn, 0)

    each((forward_u, 0))
    each((up_stream.first, 0), lo=0, hi=5)
    prepare_dy()
    each((up_stream.first, 0), lo=5, hi=CHUNKS)
    load_w(2).wait()
    send_w(2).wait_recv()
    swap_dy().wait_recv()
    each((forward_d, 0))
    each((second_u, 0))
    each((dy_stream.first, 0))
    each((third_u, 0))
    each((second_d, 0))
    each((third_d, 0))
    each((gather_a1, 0))
    each((gather_b1, 0))
    each((gather_b2, 0))
    for d in Y_ALL:
        ha1(d).start()
    hb1().start()
    each((gather_a2, 0))
    each((gather_b3, 0))
    each((backward_a, 0))
    each((backward_b, 0))
    m.gxb[0] = m.gxa[:, :, :, :HALF].astype(BF16)
    m.gxb[1] = m.gxa[:, :, :, HALF:].astype(BF16)
    tail_h().start()
    for d in Z_ORDER:
        tail_z2(d).start()
    for d in Y_ALL:
        ha1(d).wait_recv()
    ha2().start()
    hsw(0).start()
    hb1().wait_recv()
    for d in Y_ALL:
        hb2(d).start()
    tail_h().wait_recv()
    m.gs[...] = m.gxa[xh, :, :, :HALF] + m.gxr[...].astype(F32)
    m.gsb[...] = m.gs[...].astype(BF16)
    for d in Z_ORDER:
        tail_z1(d).start()
    each((backward_w, 0))
    ha2().wait_recv()
    hsw(1).start()
    for d in Y_ALL:
        hb2(d).wait_recv()
    hsw(2).start()
    total = m.gxa[:, z, :, HALF:]
    for d in Z_ORDER:
        tail_z2(d).wait_recv()
        total = total + m.gz2[d - 1].astype(F32)
    m.es[...] = total
    tail_h2().start()
    for part in range(3):
        hsw(part).wait_recv()
    each((backward_d, 0))
    total = m.gs[z]
    for d in Z_ORDER:
        tail_z1(d).wait_recv()
        total = total + m.gz1[d - 1].astype(F32)
    gx_ref[:, :HALF] = total.astype(BF16)
    tail_h2().wait_recv()
    gx_ref[:, HALF:] = (m.es[xh] + m.esr[...]).astype(BF16)

    sent = [send_w(j) for j in range(3)] + [dy_h(), swap_x(0), swap_x(1), swap_dy()]
    sent += [c(d) for c in (x_z, dy_z, tail_z1, tail_z2) for d in range(1, NZ)]
    sent += [x_h(d) for d in range(NZ)] + [tail_h(), tail_h2()]
    sent += [c(d) for c in (ha1, hb2) for d in Y_ALL] + [ha2(), hb1()] + [hsw(p) for p in range(3)]
    for c in sent:
        c.wait_send()

    def drain(i, _):
        sent = up_stream.sent(i) + dy_stream.sent(i) + [ga2(i), gb1(i)]
        sent += [ga1(i, d) for d in Y_ALL] + [g(i, w) for g in (gb2, gb3) for w in range(2)]
        sent += [sw(i, part) for part in range(3)]
        for c in sent:
            c.wait_send()
        return 0

    lax.fori_loop(0, CHUNKS, drain, 0)


def writer(gx, outs, gx_out, gg_out, gu_out, gd_out, sems):
    copies = [
        pltpu.make_async_copy(outs.at[:, :, pl.ds(ROWS * j, ROWS)], dst, sems.at[j])
        for j, dst in enumerate((gg_out, gu_out, gd_out))
    ]
    copies.append(pltpu.make_async_copy(gx, gx_out, sems.at[3]))
    for c in copies:
        c.start()
    for c in copies:
        c.wait()


def per_device(x_rows, grad_out, order, gate_t, up_t, down_w):
    any_spec = pl.BlockSpec(memory_space=pl.ANY)
    hbm_spec = pl.BlockSpec(memory_space=pltpu.HBM)
    vmem_spec = pl.BlockSpec(memory_space=pltpu.VMEM)
    dma = pltpu.SemaphoreType.DMA
    held = pl.pallas_call(
        kernel,
        out_shape=[pltpu.VMEM((TB, WIDE), BF16), pltpu.VMEM((2, CHUNKS, 3 * ROWS, WIDE), BF16)],
        in_specs=[hbm_spec, hbm_spec, vmem_spec] + [hbm_spec] * 3,
        out_specs=[vmem_spec] * 2,
        scratch_shapes=[
            dma(shape) if dtype is None else pltpu.VMEM(shape, dtype)
            for _, shape, dtype in scratch_plan()
        ],
        compiler_params=pltpu.CompilerParams(
            collective_id=0, has_side_effects=True, vmem_limit_bytes=57 * 2**20
        ),
        name="ffn_backward",
    )(
        x_rows, grad_out, order.reshape(1, TOK),
        gate_t.reshape(WEIGHT), up_t.reshape(WEIGHT), down_w.reshape(WEIGHT),
    )
    out = pl.pallas_call(
        writer,
        out_shape=[jax.ShapeDtypeStruct((TB, WIDE), BF16)]
        + [jax.ShapeDtypeStruct(WEIGHT, BF16)] * 3,
        in_specs=[vmem_spec] * 2,
        out_specs=[any_spec] * 4,
        scratch_shapes=[dma((4,))],
        compiler_params=pltpu.CompilerParams(vmem_limit_bytes=4 * 2**20),
        name="write_results",
    )(*held)
    full = gate_t.shape
    return out[0], out[1].reshape(full), out[2].reshape(full), out[3].reshape(full)


def solution(mesh):
    return jax.shard_map(
        per_device,
        mesh=mesh,
        in_specs=(
            P("tensor", "dp"),
            P("tensor", "dp"),
            P(),
            P("tensor", "dp"),
            P("tensor", "dp"),
            P("tensor", "dp"),
        ),
        out_specs=(P("tensor", "dp"), P("tensor", "dp"), P("tensor", "dp"), P("tensor", "dp")),
        check_vma=False,
    )
```

time: 555 us -> 90.7 us (0.16)
  waiting for transfers between devices: 426 us -> 0 us
  Pallas kernels: 0 us -> 90 us
  blocking collectives: 72.5 us -> 0 us
  matrix products: 21.9 us -> 0 us
  between operations: 13.8 us -> 0.64 us
  other arithmetic: 9.47 us -> 0 us
  local copies, waits for them, and re-layouts: 6.2 us -> 0 us
    reduce_scatter x2 -> x0, waiting for transfers between devices: 324 us -> none  [the longest x1 188 us: per_device(): lax.psum_scatter(stored, 'tensor', scatter_dimension=0, tiled=True)]
    all_gather x3 -> x0, waiting for transfers between devices: 101 us -> none  [the longest x1 36.1 us: per_device(): lax.all_gather(grad_pre_gate, 'dp', axis=0, tiled=True)]
    pallas_call x0 -> x2, Pallas kernels: none -> 90 us  [the longest x1 87.5 us: per_device(): pl.pallas_call(kernel, out_shape=[pltpu.VMEM((TB, WIDE), BF16), pltpu.VME...]
    all_gather x2 -> x0, blocking collectives: 72.5 us -> none  [the longest x1 40.7 us: per_device(): lax.all_gather(grad_out, 'tensor', axis=0, tiled=True)]
    dot_general x8 -> x0, matrix products: 21.9 us -> none  [the longest x3 5.02 us: times_rows(): lax.dot_general(left, weight, (((1,), (1,)), ((), ())), preferred_element...]
  transfers between devices with their start and end apart: 5 -> 0, of which waited for: 5 -> 0; matrix products, arithmetic and copies ran while one was open for 4% -> 0% of each run, Pallas kernels for 0% -> 0%
where the time goes in v2:
time: 90.7 us; the launch traced here: 90.6 us
  Pallas kernels  90 us (99%)
    pallas_call x1, Pallas kernels, per_device(): pl.pallas_call(kernel, out_shape=[pltpu.VMEM((TB, WIDE), BF16), pltpu.VME...  87.5 us
    pallas_call x1, Pallas kernels, per_device(): pl.pallas_call(writer, out_shape=[jax.ShapeDtypeStruct((TB, WIDE), BF16)]...  2.47 us

profile of v2, /device:TPU:1, one launch (start us, length us, event | category | flops | bytes accessed | tf_op | source)
XLA Modules:
  0.0 90.6 jit_solution(14722557105485170230)
XLA Ops:
  0.6 87.5 %ffn_backward.1 = (bf16[32,512]{1,0:T(8,128)(2,1)S(1)}, bf16[2,7,384,512]{3,2,1,0:T(8,128)(2,1)S(1)}) custom-call(bf16[32,512]{1,0:T(8,128)(2,1)} %x_hbm.1, bf16[32,512]{1,0:T(8,128)(2,1)} %dy_hbm.1, s32[1,512]{1,0:T(1,128)} %bitcast.10, bf16[2,7,128,512]{3,2,1,0:T(8,128)(2,1)} %bitcast.7, bf16[2,7,128,512]{3,2,1,0:T(8,128)(2,1)} %bitcast.8, ...), custom_call_target="tpu_custom_call" | custom-call | tf_op jit(solution)/shard_map/ffn_backward/pallas_call | solution.py:558
  88.1 2.5 %write_results.1 = (bf16[32,512]{1,0:T(8,128)(2,1)}, bf16[2,7,128,512]{3,2,1,0:T(8,128)(2,1)}, bf16[2,7,128,512]{3,2,1,0:T(8,128)(2,1)}, bf16[2,7,128,512]{3,2,1,0:T(8,128)(2,1)}) custom-call(bf16[32,512]{1,0:T(8,128)(2,1)S(1)} %get-tuple-element.10.gx, bf16[2,7,384,512]{3,2,1,0:T(8,128)(2,1)S(1)} %get-tuple-element.11.outs), custom_call_target="tpu_custom_call" | custom-call | tf_op jit(solution)/shard_map/write_results/pallas_call | solution.py:575

commit v3 on v2

--- a/solution.py
+++ b/solution.py
@@ -139,17 +139,17 @@
         return rc((wg, wu, wd)[j].at[1 - k], dst, m.w_send.at[j], m.w_recv.at[j], sibling)
 
     def load_x():
-        return pltpu.make_async_copy(x_hbm, m.xo.at[xh, z], m.l_sem.at[3])
+        return pltpu.make_async_copy(x_hbm, m.xo.at[0, z], m.l_sem.at[3])
 
     def load_dy():
         return pltpu.make_async_copy(dy_hbm, m.dg.at[xh, z], m.l_sem.at[4])
 
     def x_z(d):
-        return rc(x_hbm, m.xo.at[xh, z], m.xz_send.at[0, d], m.xz_recv.at[0, d], z_peer(d))
+        return rc(x_hbm, m.xo.at[0, z], m.xz_send.at[0, d], m.xz_recv.at[0, d], z_peer(d))
 
     def x_h(d):
-        block = m.xo.at[xh, (z + NZ - d) % NZ]
-        return rc(block, block, m.xh_send.at[d], m.xh_recv.at[d], h_peer)
+        at_z = (z + NZ - d) % NZ
+        return rc(m.xo.at[0, at_z], m.xo.at[1, at_z], m.xh_send.at[d], m.xh_recv.at[d], h_peer)
 
     def dy_h():
         return rc(dy_hbm, m.dg.at[xh, z], m.xh_send.at[NZ], m.xh_recv.at[NZ], h_peer)
@@ -159,8 +159,7 @@
         return rc(pair, pair, m.xz_send.at[1, d], m.xz_recv.at[1, d], z_peer(d))
 
     def swap_x(part):
-        half = (xh, 1 - xh)[part]
-        return rc(m.xo.at[half], m.xs.at[half], m.sib_send.at[part], m.sib_recv.at[part], sibling)
+        return rc(m.xo.at[part], m.xs.at[part], m.sib_send.at[part], m.sib_recv.at[part], sibling)
 
     def swap_dy():
         return rc(m.do, m.ds, m.sib_send.at[2], m.sib_recv.at[2], sibling)
@@ -189,12 +188,16 @@
         def b2(i):
             return cc(i, 8, q.sb_b.at[i], q.rx_b.at[i], x_peer)
 
-        def begin(i, parts):
-            for pf, pb, lo in ((q.pf_a, q.pb_a, 0), (q.pf_b, q.pb_b, HALF)):
-                part = parts[:, lo : lo + HALF].reshape(nf, NXL, NY, SUB, HALF)
-                pf[i] = part
-                pb[i] = part.astype(BF16)
+        def begin_a(i, part):
+            part = part.reshape(nf, NXL, NY, SUB, HALF)
+            q.pf_a[i] = part
+            q.pb_a[i] = part.astype(BF16)
             a1(i).start()
+
+        def begin_b(i, part):
+            part = part.reshape(nf, NXL, NY, SUB, HALF)
+            q.pf_b[i] = part
+            q.pb_b[i] = part.astype(BF16)
             for w in range(2):
                 b0(i, w).start()
 
@@ -235,7 +238,7 @@
             return cs + [b(i, w) for b in (b0, b1) for w in range(2)]
 
         return SimpleNamespace(
-            begin=begin, first=first, sum_a=sum_a, second_b=second_b, sum_b=sum_b, sent=sent
+            begin_a=begin_a, begin_b=begin_b, first=first, sum_a=sum_a, second_b=second_b, sum_b=sum_b, sent=sent
         )
 
     up_stream, dy_stream = stream("u", 2), stream("d", 1)
@@ -285,7 +288,7 @@
         return rc(src, dst, m.t_send.at[c], m.t_recv.at[c], dev)
 
     def tail_h():
-        return ct(0, m.gxb.at[0, 1 - xh], m.gxr, h_peer)
+        return ct(0, m.gxb.at[0, 1], m.gxr, h_peer)
 
     def tail_z1(d):
         return ct(d, m.gsb.at[(z + d) % NZ], m.gz1.at[d - 1], z_peer(d))
@@ -294,7 +297,7 @@
         return ct(NZ + d, m.gxb.at[1, :, (z + d) % NZ], m.gz2.at[d - 1], z_peer(d))
 
     def tail_h2():
-        return ct(NZ, m.es.at[1 - xh], m.esr, h_peer)
+        return ct(NZ, m.es.at[1], m.esr, h_peer)
 
     load_x().start()
     load_dy().start()
@@ -315,7 +318,7 @@
     for j in range(3):
         send_w(j).start()
     m.gxa[...] = jnp.zeros_like(m.gxa)
-    rows = lax.broadcasted_iota(jnp.int32, (TOK, TOK), 0)
+    rows = (lax.broadcasted_iota(jnp.int32, (TOK, TOK), 0) + xh * HALF) % TOK
     m.place[...] = jnp.where(rows == order_ref[...], 1.0, 0.0).astype(BF16)
     for d in Z_ORDER:
         x_z(d).wait_recv()
@@ -325,14 +328,10 @@
     dy_h().wait_recv()
     for d in Z_ORDER:
         dy_z(d).start()
-    for d in range(NZ):
-        x_h(d).wait_recv()
-    swap_x(1).start()
     for j in range(2):
         load_w(j).wait()
         send_w(j).wait_recv()
-    for part in range(2):
-        swap_x(part).wait_recv()
+    swap_x(0).wait_recv()
 
     def flat(ref):
         return ref[...].reshape(TOK, WIDE)
@@ -343,17 +342,24 @@
         m.do[...] = dot_nn(m.place[...], flat(m.dg)).astype(BF16).reshape(NXH, NZ, TB, WIDE)
         swap_dy().start()
 
-    def forward_u(i):
-        up_stream.begin(
-            i,
-            dot_nt(m.wall[k, i, : 2 * ROWS], flat(m.xo)) + dot_nt(m.wsib[i, : 2 * ROWS], flat(m.xs)),
-        )
+    def half_of(ref, p):
+        return ref[p].reshape(HALF, WIDE)
+
+    def gate_up(i, p):
+        own = dot_nt(m.wall[k, i, : 2 * ROWS], half_of(m.xo, p))
+        return own + dot_nt(m.wsib[i, : 2 * ROWS], half_of(m.xs, p))
+
+    def forward_ua(i):
+        up_stream.begin_a(i, gate_up(i, 0))
+
+    def forward_ub(i):
+        up_stream.begin_b(i, gate_up(i, 1))
 
     def forward_d(i):
-        dy_stream.begin(
-            i,
-            dot_nt(m.wall[k, i, 2 * ROWS :], flat(m.do)) + dot_nt(m.wsib[i, 2 * ROWS :], flat(m.ds)),
-        )
+        own = dot_nt(m.wall[k, i, 2 * ROWS :], flat(m.do))
+        both = own + dot_nt(m.wsib[i, 2 * ROWS :], flat(m.ds))
+        dy_stream.begin_a(i, both[:, :HALF])
+        dy_stream.begin_b(i, both[:, HALF:])
 
     def hidden_of(i, total, t, h):
         t[i] = total
@@ -457,7 +463,12 @@
 
         lax.fori_loop(lo, hi + most, turn, 0)
 
-    each((forward_u, 0))
+    each((forward_ua, 0))
+    for d in range(NZ):
+        x_h(d).wait_recv()
+    swap_x(1).start()
+    swap_x(1).wait_recv()
+    each((forward_ub, 0))
     each((up_stream.first, 0), lo=0, hi=5)
     prepare_dy()
     each((up_stream.first, 0), lo=5, hi=CHUNKS)
@@ -469,15 +480,22 @@
     each((dy_stream.first, 0))
     each((third_u, 0))
     each((second_d, 0))
+    for d in Y_ALL:
+        ha1(d).start()
     each((third_d, 0))
     each((gather_a1, 0))
+    hb1().start()
     each((gather_b1, 0))
     each((gather_b2, 0))
-    for d in Y_ALL:
-        ha1(d).start()
-    hb1().start()
     each((gather_a2, 0))
     each((gather_b3, 0))
+    for d in Y_ALL:
+        ha1(d).wait_recv()
+    ha2().start()
+    hsw(0).start()
+    hb1().wait_recv()
+    for d in Y_ALL:
+        hb2(d).start()
     each((backward_a, 0))
     each((backward_b, 0))
     m.gxb[0] = m.gxa[:, :, :, :HALF].astype(BF16)
@@ -485,15 +503,8 @@
     tail_h().start()
     for d in Z_ORDER:
         tail_z2(d).start()
-    for d in Y_ALL:
-        ha1(d).wait_recv()
-    ha2().start()
-    hsw(0).start()
-    hb1().wait_recv()
-    for d in Y_ALL:
-        hb2(d).start()
     tail_h().wait_recv()
-    m.gs[...] = m.gxa[xh, :, :, :HALF] + m.gxr[...].astype(F32)
+    m.gs[...] = m.gxa[0, :, :, :HALF] + m.gxr[...].astype(F32)
     m.gsb[...] = m.gs[...].astype(BF16)
     for d in Z_ORDER:
         tail_z1(d).start()
@@ -518,7 +529,7 @@
         total = total + m.gz1[d - 1].astype(F32)
     gx_ref[:, :HALF] = total.astype(BF16)
     tail_h2().wait_recv()
-    gx_ref[:, HALF:] = (m.es[xh] + m.esr[...]).astype(BF16)
+    gx_ref[:, HALF:] = (m.es[0] + m.esr[...]).astype(BF16)
 
     sent = [send_w(j) for j in range(3)] + [dy_h(), swap_x(0), swap_x(1), swap_dy()]
     sent += [c(d) for c in (x_z, dy_z, tail_z1, tail_z2) for d in range(1, NZ)]

time: 90.7 us -> 89 us (0.981)
  Pallas kernels: 90 us -> 88 us
    pallas_call x1, Pallas kernels: 87.5 us -> 85.5 us  [per_device(): pl.pallas_call(kernel, out_shape=[pltpu.VMEM((TB, WIDE), BF16), pltpu.VME...]
where the time goes in v3:
time: 89 us; the launch traced here: 88.6 us
  Pallas kernels  88 us (99%)
    pallas_call x1, Pallas kernels, per_device(): pl.pallas_call(kernel, out_shape=[pltpu.VMEM((TB, WIDE), BF16), pltpu.VME...  85.5 us
    pallas_call x1, Pallas kernels, per_device(): pl.pallas_call(writer, out_shape=[jax.ShapeDtypeStruct((TB, WIDE), BF16)]...  2.47 us

profile of v3, /device:TPU:1, one launch (start us, length us, event | category | flops | bytes accessed | tf_op | source)
XLA Modules:
  0.0 88.6 jit_solution(12183740686953497960)
XLA Ops:
  0.6 85.5 %ffn_backward.1 = (bf16[32,512]{1,0:T(8,128)(2,1)S(1)}, bf16[2,7,384,512]{3,2,1,0:T(8,128)(2,1)S(1)}) custom-call(bf16[32,512]{1,0:T(8,128)(2,1)} %x_hbm.1, bf16[32,512]{1,0:T(8,128)(2,1)} %dy_hbm.1, s32[1,512]{1,0:T(1,128)} %bitcast.10, bf16[2,7,128,512]{3,2,1,0:T(8,128)(2,1)} %bitcast.7, bf16[2,7,128,512]{3,2,1,0:T(8,128)(2,1)} %bitcast.8, ...), custom_call_target="tpu_custom_call" | custom-call | tf_op jit(solution)/shard_map/ffn_backward/pallas_call | solution.py:569
  86.2 2.5 %write_results.1 = (bf16[32,512]{1,0:T(8,128)(2,1)}, bf16[2,7,128,512]{3,2,1,0:T(8,128)(2,1)}, bf16[2,7,128,512]{3,2,1,0:T(8,128)(2,1)}, bf16[2,7,128,512]{3,2,1,0:T(8,128)(2,1)}) custom-call(bf16[32,512]{1,0:T(8,128)(2,1)S(1)} %get-tuple-element.10.gx, bf16[2,7,384,512]{3,2,1,0:T(8,128)(2,1)S(1)} %get-tuple-element.11.outs), custom_call_target="tpu_custom_call" | custom-call | tf_op jit(solution)/shard_map/write_results/pallas_call | solution.py:586

commit v4 on v3

--- a/solution.py
+++ b/solution.py
@@ -115,14 +115,20 @@
     x_peer = at(y, 1 - xl, k, xh, z)
     h_peer = at(y, xl, k, 1 - xh, z)
 
+    other = 1 - xl
+    y_row = [lax.rem(y + d, NY) for d in range(NY)]
+    y_dev = [at(row, xl, k, xh, z) for row in y_row]
+    z_row = [lax.rem(z + d, NZ) for d in range(NZ)]
+    z_dev = [at(y, xl, k, xh, row) for row in z_row]
+
     def y_at(d):
-        return (y + d) % NY
+        return y_row[d % NY]
 
     def y_peer(d):
-        return at(y_at(d), xl, k, xh, z)
+        return y_dev[d % NY]
 
     def z_peer(d):
-        return at(y, xl, k, xh, (z + d) % NZ)
+        return z_dev[d % NZ]
 
     def rc(src, dst, send, recv, dev):
         return pltpu.make_async_remote_copy(
@@ -148,7 +154,7 @@
         return rc(x_hbm, m.xo.at[0, z], m.xz_send.at[0, d], m.xz_recv.at[0, d], z_peer(d))
 
     def x_h(d):
-        at_z = (z + NZ - d) % NZ
+        at_z = z_row[(NZ - d) % NZ]
         return rc(m.xo.at[0, at_z], m.xo.at[1, at_z], m.xh_send.at[d], m.xh_recv.at[d], h_peer)
 
     def dy_h():
@@ -174,7 +180,7 @@
             return rc(src, dst, q.send.at[i, c], q.recv.at[i, c], dev)
 
         def a1(i):
-            return cc(i, 0, q.pb_a.at[i, :, 1 - xl], q.rx_a.at[i], x_peer)
+            return cc(i, 0, q.pb_a.at[i, :, other], q.rx_a.at[i], x_peer)
 
         def a2(i, d):
             return cc(i, d, q.sb_a.at[i, :, y_at(d)], q.ry_a.at[i, d - 1], y_peer(d))
@@ -202,16 +208,16 @@
                 b0(i, w).start()
 
         def first(i):
+            a1(i).wait_recv()
+            q.sb_a[i] = (q.pf_a[i, :, xl] + q.rx_a[i].astype(F32)).astype(BF16)
+            for d in Y_ALL:
+                a2(i, d).start()
             for w in range(2):
                 b0(i, w).wait_recv()
                 to = y_at((1, 3)[w])
                 q.f_b[i, w, :, w] = (q.pf_b[i, :, w, to] + q.r0_b[i, w].astype(F32)).astype(BF16)
                 q.f_b[i, w, :, 1 - w] = q.pb_b[i, :, 1 - w, to]
                 b1(i, w).start()
-            a1(i).wait_recv()
-            q.sb_a[i] = (q.pf_a[i, :, xl] + q.rx_a[i].astype(F32)).astype(BF16)
-            for d in Y_ALL:
-                a2(i, d).start()
 
         def sum_a(i):
             total = q.pf_a[i, :, xl, y] + q.rx_a[i, :, y].astype(F32)
@@ -226,7 +232,7 @@
                 b1(i, w).wait_recv()
                 total = total + q.r1_b[i, w].astype(F32)
             q.s_b[i] = total
-            q.sb_b[i] = q.s_b[i, :, 1 - xl].astype(BF16)
+            q.sb_b[i] = q.s_b[i, :, other].astype(BF16)
             b2(i).start()
 
         def sum_b(i):
@@ -262,7 +268,7 @@
         return cg(i, 7 + w, m.g_b.at[k, i, :, w, y_at((3, 1)[w])], y_peer((1, 3)[w]))
 
     def sw(i, part):
-        src = (m.g_a.at[k, i, :, xl], m.g_a.at[k, i, :, 1 - xl], m.g_b.at[k, i])[part]
+        src = (m.g_a.at[k, i, :, xl], m.g_a.at[k, i, :, other], m.g_b.at[k, i])[part]
         return cg(i, 9 + part, src, sibling)
 
     def ch(c, src, dev):
@@ -281,7 +287,7 @@
         return ch(4 + d, m.h_b.at[k, :, :, y], y_peer(d))
 
     def hsw(part):
-        src = (m.h_a.at[k, :, xl], m.h_a.at[k, :, 1 - xl], m.h_b.at[k])[part]
+        src = (m.h_a.at[k, :, xl], m.h_a.at[k, :, other], m.h_b.at[k])[part]
         return ch(8 + part, src, sibling)
 
     def ct(c, src, dst, dev):
@@ -291,10 +297,10 @@
         return ct(0, m.gxb.at[0, 1], m.gxr, h_peer)
 
     def tail_z1(d):
-        return ct(d, m.gsb.at[(z + d) % NZ], m.gz1.at[d - 1], z_peer(d))
+        return ct(d, m.gsb.at[z_row[d]], m.gz1.at[d - 1], z_peer(d))
 
     def tail_z2(d):
-        return ct(NZ + d, m.gxb.at[1, :, (z + d) % NZ], m.gz2.at[d - 1], z_peer(d))
+        return ct(NZ + d, m.gxb.at[1, :, z_row[d]], m.gz2.at[d - 1], z_peer(d))
 
     def tail_h2():
         return ct(NZ, m.es.at[1], m.esr, h_peer)
@@ -382,10 +388,10 @@
         g[k, i, 1, xl, y] = grad_up.astype(BF16)
 
     def second_d(i):
+        dy_stream.second_b(i)
         gated(i, dy_stream.sum_a(i)[0], m.t_a, m.g_a)
         for d in Y_ALL:
             ga1(i, d).start()
-        dy_stream.second_b(i)
 
     def third_d(i):
         gated(i, dy_stream.sum_b(i)[0], m.t_b, m.g_b)
@@ -417,10 +423,8 @@
         sw(i, 2).start()
 
     def backward(i, p, g):
-        for h in range(2):
-            m.gxa[p] += dot_tn(
-                g[h, i].reshape(2 * ROWS, HALF), m.wall[h, i, : 2 * ROWS]
-            ).reshape(NZ, TB, WIDE)
+        both = [dot_tn(g[h, i].reshape(2 * ROWS, HALF), m.wall[h, i, : 2 * ROWS]) for h in range(2)]
+        m.gxa[p] += (both[0] + both[1]).reshape(NZ, TB, WIDE)
 
     def backward_a(i):
         for part in range(2):
@@ -462,6 +466,22 @@
             return 0
 
         lax.fori_loop(lo, hi + most, turn, 0)
+
+    def drain(i, _):
+        sent = up_stream.sent(i) + dy_stream.sent(i) + [ga2(i), gb1(i)]
+        sent += [ga1(i, d) for d in Y_ALL] + [g(i, w) for g in (gb2, gb3) for w in range(2)]
+        sent += [sw(i, part) for part in range(3)]
+        for c in sent:
+            c.wait_send()
+        return 0
+
+    def drain_all():
+        sent = [send_w(j) for j in range(3)] + [dy_h(), swap_x(0), swap_x(1), swap_dy()]
+        sent += [c(d) for c in (x_z, dy_z) for d in range(1, NZ)] + [x_h(d) for d in range(NZ)]
+        sent += [ha1(d) for d in Y_ALL] + [ha2(), hb1()]
+        for c in sent:
+            c.wait_send()
+        lax.fori_loop(0, CHUNKS, drain, 0)
 
     each((forward_ua, 0))
     for d in range(NZ):
@@ -514,6 +534,7 @@
     for d in Y_ALL:
         hb2(d).wait_recv()
     hsw(2).start()
+    drain_all()
     total = m.gxa[:, z, :, HALF:]
     for d in Z_ORDER:
         tail_z2(d).wait_recv()
@@ -531,22 +552,10 @@
     tail_h2().wait_recv()
     gx_ref[:, HALF:] = (m.es[0] + m.esr[...]).astype(BF16)
 
-    sent = [send_w(j) for j in range(3)] + [dy_h(), swap_x(0), swap_x(1), swap_dy()]
-    sent += [c(d) for c in (x_z, dy_z, tail_z1, tail_z2) for d in range(1, NZ)]
-    sent += [x_h(d) for d in range(NZ)] + [tail_h(), tail_h2()]
-    sent += [c(d) for c in (ha1, hb2) for d in Y_ALL] + [ha2(), hb1()] + [hsw(p) for p in range(3)]
+    sent = [c(d) for c in (tail_z1, tail_z2) for d in range(1, NZ)] + [tail_h(), tail_h2()]
+    sent += [hb2(d) for d in Y_ALL] + [hsw(p) for p in range(3)]
     for c in sent:
         c.wait_send()
-
-    def drain(i, _):
-        sent = up_stream.sent(i) + dy_stream.sent(i) + [ga2(i), gb1(i)]
-        sent += [ga1(i, d) for d in Y_ALL] + [g(i, w) for g in (gb2, gb3) for w in range(2)]
-        sent += [sw(i, part) for part in range(3)]
-        for c in sent:
-            c.wait_send()
-        return 0
-
-    lax.fori_loop(0, CHUNKS, drain, 0)
 
 
 def writer(gx, outs, gx_out, gg_out, gu_out, gd_out, sems):

time: 89 us -> 88.2 us (level)
  no operation moved by 1% of the time
where the time goes in v4:
time: 88.2 us; the launch traced here: 88.1 us
  Pallas kernels  87.5 us (99%)
    pallas_call x1, Pallas kernels, per_device(): pl.pallas_call(kernel, out_shape=[pltpu.VMEM((TB, WIDE), BF16), pltpu.VME...  85 us
    pallas_call x1, Pallas kernels, per_device(): pl.pallas_call(writer, out_shape=[jax.ShapeDtypeStruct((TB, WIDE), BF16)]...  2.47 us

profile of v4, /device:TPU:1, one launch (start us, length us, event | category | flops | bytes accessed | tf_op | source)
XLA Modules:
  0.0 88.1 jit_solution(1964098330308617353)
XLA Ops:
  0.6 85.0 %ffn_backward.1 = (bf16[32,512]{1,0:T(8,128)(2,1)S(1)}, bf16[2,7,384,512]{3,2,1,0:T(8,128)(2,1)S(1)}) custom-call(bf16[32,512]{1,0:T(8,128)(2,1)} %x_hbm.1, bf16[32,512]{1,0:T(8,128)(2,1)} %dy_hbm.1, s32[1,512]{1,0:T(1,128)} %bitcast.10, bf16[2,7,128,512]{3,2,1,0:T(8,128)(2,1)} %bitcast.7, bf16[2,7,128,512]{3,2,1,0:T(8,128)(2,1)} %bitcast.8, ...), custom_call_target="tpu_custom_call" | custom-call | tf_op jit(solution)/shard_map/ffn_backward/pallas_call | solution.py:578
  85.7 2.5 %write_results.1 = (bf16[32,512]{1,0:T(8,128)(2,1)}, bf16[2,7,128,512]{3,2,1,0:T(8,128)(2,1)}, bf16[2,7,128,512]{3,2,1,0:T(8,128)(2,1)}, bf16[2,7,128,512]{3,2,1,0:T(8,128)(2,1)}) custom-call(bf16[32,512]{1,0:T(8,128)(2,1)S(1)} %get-tuple-element.10.gx, bf16[2,7,384,512]{3,2,1,0:T(8,128)(2,1)S(1)} %get-tuple-element.11.outs), custom_call_target="tpu_custom_call" | custom-call | tf_op jit(solution)/shard_map/write_results/pallas_call | solution.py:595
